TPU v7x, 256 devices: a whole 4x4x8 slice. The times are simulated.
256 devices in a mesh: dp: 8 (over x, core), tp: 32 (over y, z).
Axes of the slice: x: 4, y: 4, z: 8, core: 2. Of those that a mesh axis runs over, the one named last changes fastest.
Arguments:
- queries: bfloat16 [2048, 64, 576], P(('dp', 'tp')), may hold values from -40 to 40
- new_key: bfloat16 [2048, 576], P(('dp', 'tp')), may hold values from -8 to 8
- latent_cache: bfloat16 [786432, 576], P(('dp', 'tp')), may hold values from -8 to 8
- lengths: int32 [2048], P(('dp', 'tp')), may hold values from 1 to 3072, as said below
- counts: int32 [256], P(('dp', 'tp')), may hold values from 1 to 8, as said below
- residual: float32 [2048, 3584], P(('dp', 'tp')), may hold values from -4 to 4
- value_up: bfloat16 [64, 512, 128], P('tp'), may hold values from -0.25 to 0.25
- output_proj: bfloat16 [8192, 3584], P('tp'), may hold values from -0.0625 to 0.0625
- norm_gain: bfloat16 [3584], replicated, may hold values from 0.5 to 2
- gate_up: bfloat16 [2, 3584, 9216], P(None, 'dp', 'tp'), may hold values from -0.09375 to 0.09375
- down_proj: bfloat16 [9216, 3584], P('tp'), may hold values from -0.0625 to 0.0625
Outputs:
- mixed: bfloat16 [2048, 3584], P(('dp', 'tp'))
Inputs may be any that keep to these rules, and one draw needn't show every extreme that they name: Slots 0 to counts - 1 of a device are live; in every draw some device has all 8 live. `lengths`: the live slots of one device hold together at most 3072 cached tokens, exactly 3072 on some device of every draw; entries of slots that are not live are stale.
All inputs are finite; a program needn't handle non-finite values.
Results may differ from a plain program's by a relative error of at most 0.014.
Values may be sent and summed in bfloat16 or wider, within the bound.
No kernel may reach another device: no remote copies, remote signals or barrier semaphores. Data moves between devices by JAX's collectives and lax.ppermute only.
A program may use at most 128 MiB of HBM per device.

v0:
```python
import jax
import jax.numpy as jnp
from jax import lax
from jax.sharding import PartitionSpec as P

SOFTMAX_SCALE = 192.0 ** (-0.5)
NORM_EPS = 1e-06


def rms_norm(rows_in, norm_gain):
    mean_square = jnp.mean(rows_in * rows_in, axis=-1, keepdims=True)
    return (rows_in * lax.rsqrt(mean_square + NORM_EPS) * norm_gain.astype(jnp.float32)).astype(
        jnp.bfloat16
    )


def local(
    queries,
    new_key,
    latent_cache,
    lengths,
    counts,
    residual,
    value_up,
    output_proj,
    norm_gain,
    gate_up,
    down_proj,
):
    slot_count, head_count, key_width = queries.shape
    latent_width = value_up.shape[1]
    pool_rows = latent_cache.shape[0]
    block_rows = min(512, pool_rows)
    slot_ids = jnp.arange(slot_count, dtype=jnp.int32)
    live_mask = slot_ids < counts[0]
    used_lengths = jnp.where(live_mask, lengths, 0)
    start_rows = jnp.cumsum(used_lengths) - used_lengths
    end_rows = start_rows + used_lengths
    total_used = jnp.sum(used_lengths)
    query_rows = queries.reshape(slot_count * head_count, key_width)
    own_score = (
        jnp.einsum("shk,sk->sh", queries, new_key, preferred_element_type=jnp.float32).reshape(-1)
        * SOFTMAX_SCALE
    )

    def block_scores(block_index):
        first_row = block_index * block_rows
        block_keys = lax.dynamic_slice_in_dim(latent_cache, first_row, block_rows, 0)
        scores = (
            lax.dot_general(
                query_rows, block_keys, (((1,), (1,)), ((), ())), preferred_element_type=jnp.float32
            )
            * SOFTMAX_SCALE
        )
        positions = first_row + jnp.arange(block_rows, dtype=jnp.int32)
        inside = (positions[None, :] >= start_rows[:, None]) & (
            positions[None, :] < end_rows[:, None]
        )
        inside = jnp.broadcast_to(inside[:, None, :], (slot_count, head_count, block_rows)).reshape(
            -1, block_rows
        )
        return (block_keys, scores, inside)

    def block_top(block_index, running_max):
        block_keys, scores, inside = block_scores(block_index)
        return jnp.maximum(running_max, jnp.max(jnp.where(inside, scores, -jnp.inf), axis=1))

    block_total = (total_used + block_rows - 1) // block_rows
    top_score = lax.fori_loop(0, block_total, block_top, own_score)
    own_prob = jnp.exp(own_score - top_score)
    own_round = own_prob.astype(jnp.bfloat16)
    start_out = own_round.reshape(slot_count, head_count)[:, :, None].astype(jnp.float32) * new_key[
        :, None, :latent_width
    ].astype(jnp.float32)
    start_out = start_out.reshape(slot_count * head_count, latent_width)

    def attend_block(block_index, carry):
        running_sum, running_out = carry
        block_keys, scores, inside = block_scores(block_index)
        probs = jnp.where(
            inside, jnp.exp(jnp.where(inside, scores, top_score[:, None]) - top_score[:, None]), 0.0
        )
        new_sum = running_sum + jnp.sum(probs, axis=1)
        new_out = running_out + jnp.dot(
            probs.astype(jnp.bfloat16),
            block_keys[:, :latent_width],
            preferred_element_type=jnp.float32,
        )
        return (new_sum, new_out)

    final_sum, final_out = lax.fori_loop(0, block_total, attend_block, (own_prob, start_out))
    latent_out = (
        (final_out / final_sum[:, None])
        .astype(jnp.bfloat16)
        .reshape(slot_count, head_count, latent_width)
    )
    head_rows = lax.all_to_all(latent_out, "tp", split_axis=1, concat_axis=0, tiled=True)
    values = jnp.einsum(
        "rhc,hcj->rhj", head_rows, value_up, preferred_element_type=jnp.float32
    ).astype(jnp.bfloat16)
    values = values.reshape(values.shape[0], values.shape[1] * values.shape[2])
    my_rank = lax.axis_index("tp")
    own_first = my_rank * slot_count
    terms = jnp.dot(values, output_proj, preferred_element_type=jnp.float32)
    own_block = lax.dynamic_slice_in_dim(terms, own_first, slot_count, 0) + residual
    terms = lax.dynamic_update_slice_in_dim(terms, own_block, own_first, 0)
    whole_state = lax.psum(terms, "tp")
    state_own = lax.dynamic_slice_in_dim(whole_state, own_first, slot_count, 0)
    normed_all = rms_norm(whole_state, norm_gain)
    piece = lax.all_gather(gate_up, "dp", axis=1, tiled=True)
    gate_part = jnp.dot(normed_all, piece[0], preferred_element_type=jnp.float32)
    upward_part = jnp.dot(normed_all, piece[1], preferred_element_type=jnp.float32)
    hidden = (jax.nn.silu(gate_part) * upward_part).astype(jnp.bfloat16)
    piece = hidden
    mixed = (
        lax.psum_scatter(
            jnp.dot(piece, down_proj, preferred_element_type=jnp.float32),
            "tp",
            scatter_dimension=0,
            tiled=True,
        )
        + state_own
    )
    return jnp.where(live_mask[:, None], mixed, 0.0).astype(jnp.bfloat16)


def solution(mesh):
    placed = (
        P(("dp", "tp"), None, None),
        P(("dp", "tp"), None),
        P(("dp", "tp"), None),
        P(("dp", "tp")),
        P(("dp", "tp")),
        P(("dp", "tp"), None),
        P("tp", None, None),
        P("tp", None),
        P(),
        P(None, "dp", "tp"),
        P("tp", None),
    )
    return jax.shard_map(
        local, mesh=mesh, in_specs=placed, out_specs=P(("dp", "tp"), None), check_vma=False
    )
```

profile of v0, /device:TPU:2, one launch (start us, length us, event | category | flops | bytes accessed | tf_op | source)
XLA Modules:
  0.0 524.3 jit_solution(8785979459662549079)
XLA Ops:
  13.2 15.0 %while.22 = (s32[]{:T(128)}, f32[512]{0:T(512)S(1)}, s32[]{:T(128)}, s32[8]{0:T(128)S(1)}, s32[8]{0:T(128)S(1)}, /*index=5*/bf16[3072,576]{0,1:T(8,128)(2,1)}, b...) while((s32[]{:T(128)}, f32[512]{0:T(512)S(1)}, s32[]{:T(128)}, ...), condition=%wide.region_4.5_spmd, body=%wide.region_2.4_spmd.sunk | while | flops 302789120 | bytes 2314475 | solution.py:69
  13.7 1.9 fusion.61
  16.2 1.9 fusion.61
  18.7 1.9 fusion.61
  23.7 1.9 fusion.61
  26.2 1.9 fusion.61
  28.3 25.4 %while.23 = (s32[]{:T(128)}, f32[512]{0:T(512)S(1)}, f32[512,512]{1,0:T(8,128)S(1)}, s32[]{:T(128)}, s32[8]{0:T(128)S(1)}, /*index=5*/s32[8]{0:T(128)S(1)}, bf16...) while((s32[]{:T(128)}, f32[512]{0:T(512)S(1)}, ...), condition=%wide.region_7.8_spmd, body=%wide.region_5.7_spmd.sunk | while | flops 572273152 | bytes 5986559 | solution.py:91
  28.9 2.1 fusion.65
  33.1 2.1 fusion.65
  37.4 2.1 fusion.65
  41.6 2.1 fusion.65
  45.8 2.1 fusion.65
  50.1 2.1 fusion.65
  55.0 10.0 %all-to-all-start = ((bf16[8,64,512]{2,0,1:T(8,128)(2,1)}), bf16[8,64,512]{2,0,1:T(8,128)(2,1)S(1)}, u32[]{:S(2)}, u32[]{:S(2)}) async-start(bf16[8,64,512]{2,0,1:T(8,128)(2,1)} %copy.34), calls=%async_computation | async-start | bytes 1048576 | tf_op jit(solution)/shard_map/all_to_all | solution.py:97
  65.0 17.6 %all-to-all-done = bf16[8,64,512]{2,0,1:T(8,128)(2,1)S(1)} async-done(((bf16[8,64,512]{2,0,1:T(8,128)(2,1)}), bf16[8,64,512]{2,0,1:T(8,128)(2,1)S(1)}, u32[]{:S(2)}, u32[]{:S(2)}) %all-to-all-start) | async-done | bytes 524320 | tf_op jit(solution)/shard_map/all_to_all | solution.py:97
  82.9 4.1 fusion.43
  90.7 156.3 %all-reduce.2.cloned.1.call-done = f32[256,3584]{1,0:T(8,128)} async-done(((f32[256,3584]{1,0:T(8,128)}), f32[256,3584]{1,0:T(8,128)}) %all-reduce.2.cloned.1.call-update) | async-done | bytes 3670032 | tf_op jit(solution)/shard_map/psum | solution.py:107
  247.0 2.4 multiply_reduce_fusion
  249.4 12.4 %fusion.42 = (bf16[1,3584,288]{2,0,1:T(2,128)(2,1)}, bf16[1,3584,288]{2,0,1:T(2,128)(2,1)}) fusion(bf16[2,3584,288]{2,0,1:T(2,128)(2,1)} %all-gather.2.cloned.1.call-done), kind=kLoop, calls=%fused_computation.58 | loop fusion | bytes 8257536 | tf_op jit(solution)/shard_map/slice | solution.py:111
  261.8 12.1 %copy.44 = bf16[1,3584,288]{1,2,0:T(8,128)(2,1)} copy(bf16[1,3584,288]{2,0,1:T(2,128)(2,1)} %get-tuple-element.132) | data formatting | bytes 4128768
  273.9 12.1 %copy.43 = bf16[1,3584,288]{1,2,0:T(8,128)(2,1)} copy(bf16[1,3584,288]{2,0,1:T(2,128)(2,1)} %get-tuple-element.131) | data formatting | bytes 4128768
  286.0 3.5 fusion.17
  289.6 7.5 %fusion.26 = f32[256,3584]{1,0:T(8,128)} fusion(bf16[288,3584]{1,0:T(8,128)(2,1)S(1)} %copy-done, bf16[1,3584,288]{1,2,0:T(8,128)(2,1)} %copy.44, f32[256,288]{0,1:T(8,128)S(1)} %fusion.17, f32[256,3584]{1,0:T(8,128)} %all-reduce.2.cloned.1.call-done, f32[3584]{0:T(1024)S(1)} %convert_element_type.45, f32[256]{0:T(256)S(1)} %add_rsqrt_fusion), kind=kOutput, calls=%fused_computation.31 | convolution fusion | flops 1060159488 | bytes 11779072 | tf_op jit(solution)/shard_map/dot_general | solution.py:117
  297.1 218.1 %reduce-scatter.2.cloned.1.call-done = f32[8,3584]{1,0:T(8,128)} async-done(((f32[256,3584]{1,0:T(8,128)}), f32[8,3584]{1,0:T(8,128)}) %reduce-scatter.2.cloned.1.call-update) | async-done | bytes 114704 | tf_op jit(solution)/shard_map/reduce_scatter | solution.py:116
  (103 shorter events, 28.8 us)
Async XLA Ops:
  7.4 282.2 %copy-start = (bf16[288,3584]{1,0:T(8,128)(2,1)S(1)}, bf16[288,3584]{1,0:T(8,128)(2,1)}, u32[]{:S(2)}) copy-start(bf16[288,3584]{1,0:T(8,128)(2,1)} %param.25) | copy-start | bytes 6193156
  53.7 28.9 %copy-start.4 = (bf16[2,512,128]{2,1,0:T(8,128)(2,1)S(1)}, bf16[2,512,128]{2,1,0:T(8,128)(2,1)}, u32[]{:S(2)}) copy-start(bf16[2,512,128]{2,1,0:T(8,128)(2,1)} %param.21) | copy-start | bytes 786436
  55.0 32.1 %copy-start.2 = (f32[8,3584]{1,0:T(8,128)S(1)}, f32[8,3584]{1,0:T(8,128)}, u32[]{:S(2)}) copy-start(f32[8,3584]{1,0:T(8,128)} %param.20) | copy-start | bytes 344068
  55.0 27.6 %all-to-all-start = ((bf16[8,64,512]{2,0,1:T(8,128)(2,1)}), bf16[8,64,512]{2,0,1:T(8,128)(2,1)S(1)}, u32[]{:S(2)}, u32[]{:S(2)}) async-start(bf16[8,64,512]{2,0,1:T(8,128)(2,1)} %copy.34), calls=%async_computation | async-start | bytes 1048576 | tf_op jit(solution)/shard_map/all_to_all | solution.py:97
  65.0 182.0 %all-reduce.2.cloned.1.call-start = ((), (), s32[]{:S(2)}) async-start(), calls=%async_computation.2 | async-start | bytes 7340032 | tf_op jit(solution)/shard_map/psum | solution.py:107
  82.9 5.8 %copy-start.1 = (bf16[2,448,288]{1,2,0:T(8,128)(2,1)S(1)}, bf16[2,448,288]{1,2,0:T(8,128)(2,1)}, u32[]{:S(2)}) copy-start(bf16[2,448,288]{1,2,0:T(8,128)(2,1)} %param.24) | copy-start | bytes 1548292
  87.0 3.6 copy-start.3
  88.7 160.7 %all-gather.2.cloned.1.call-start = ((), (), s32[]{:S(2)}) async-start(), calls=%async_computation.3 | async-start | bytes 6193152 | tf_op jit(solution)/shard_map/all_gather | solution.py:110
  90.6 424.6 %reduce-scatter.2.cloned.1.call-start = ((), (), s32[]{:S(2)}) async-start(), calls=%async_computation.4 | async-start | bytes 3784704 | tf_op jit(solution)/shard_map/reduce_scatter | solution.py:116
Sparse Core Ops, SparseCore 0:
  88.8 158.1 all-reduce.1
  297.2 217.9 reduce-scatter.1
Sparse Core Ops, SparseCore 1:
  91.0 36.5 all-gather.1
where the time goes:
time: 526 us; the launch traced here: 524 us
  waiting for transfers between devices  392 us (75%)
  matrix products  50.4 us (10%)
  local copies, waits for them, and re-layouts  44.8 us (9%)
  between operations  16.4 us (3%)
  starting transfers between devices  10.1 us (2%)
  other arithmetic  9.87 us (2%)
    reduce_scatter x1, waiting for transfers between devices, local(): lax.psum_scatter(jnp.dot(piece, down_proj, preferred_element_type=jnp.flo...  218 us
    psum x1, waiting for transfers between devices, local(): whole_state = lax.psum(terms, 'tp')  156 us
    unnamed x14, local copies, waits for them, and re-layouts  26.1 us
    dot_general x12, matrix products, block_scores(): lax.dot_general(query_rows, block_keys, (((1,), (1,)), ((), ())), preferr...  24.3 us
    all_to_all x1, waiting for transfers between devices, local(): lax.all_to_all(latent_out, 'tp', split_axis=1, concat_axis=0, tiled=True)  17.6 us
    slice x1, local copies, waits for them, and re-layouts, local(): piece[0]  12.4 us
  transfers between devices with their start and end apart: 4, of which 3 were waited for; matrix products, arithmetic and copies ran while one was open for 1% of the time, Pallas kernels for 0%

commit v1 on v0

v1 whole, which is shorter than its diff:
```python
import functools

import jax
import jax.numpy as jnp
from jax import lax
from jax.experimental import pallas as pl
from jax.experimental.pallas import tpu as pltpu
from jax.sharding import PartitionSpec as P

SOFTMAX_SCALE = 192.0 ** (-0.5)
NORM_EPS = 1e-06
Y_SIZE = 4
Z_SIZE = 8
BLOCK = 512
Z_GROUPS = [[y * Z_SIZE + z for z in range(Z_SIZE)] for y in range(Y_SIZE)]
BF16 = jnp.bfloat16
F32 = jnp.float32
VMEM = pl.BlockSpec(memory_space=pltpu.VMEM)
SMEM = pl.BlockSpec(memory_space=pltpu.SMEM)
PARAMS = pltpu.CompilerParams(vmem_limit_bytes=40 * 1024 * 1024)


def y_shift(array, step):
    pairs = [
        (y * Z_SIZE + z, ((y + step) % Y_SIZE) * Z_SIZE + z)
        for y in range(Y_SIZE)
        for z in range(Z_SIZE)
    ]
    return lax.ppermute(array, "tp", pairs)


def z_exchange(array):
    return lax.all_to_all(
        array, "tp", split_axis=0, concat_axis=0, tiled=True, axis_index_groups=Z_GROUPS
    )


def attend_kernel(bounds_ref, query_ref, new_key_ref, keys_ref, out_ref, acc_ref):
    slots, heads = 8, 64
    latent = out_ref.shape[1]
    for pair in range(slots // 2):
        first = 2 * pair
        rows = pl.ds(first * heads, 2 * heads)
        query = query_ref[rows, :]
        own_rows = []
        for s in (first, first + 1):
            own_rows.append(
                jnp.broadcast_to(new_key_ref[s : s + 1, :].astype(F32), (heads, query.shape[1]))
            )
        own_keys = jnp.concatenate(own_rows, axis=0)
        own_score = (
            jnp.sum(query.astype(F32) * own_keys, axis=1, keepdims=True) * SOFTMAX_SCALE
        )
        acc_ref[...] = own_keys[:, :latent]
        is_second = lax.broadcasted_iota(jnp.int32, (2 * heads, 1), 0) >= heads
        row_start = jnp.where(is_second, bounds_ref[first + 1], bounds_ref[first])
        row_end = jnp.where(is_second, bounds_ref[first + 2], bounds_ref[first + 1])
        begin = bounds_ref[first] // BLOCK
        end = (bounds_ref[first + 2] + BLOCK - 1) // BLOCK

        def step(block, carry):
            top, total = carry
            offset = pl.multiple_of(block * BLOCK, BLOCK)
            scores = (
                jnp.dot(query, keys_ref[:, pl.ds(offset, BLOCK)], preferred_element_type=F32)
                * SOFTMAX_SCALE
            )
            positions = offset + lax.broadcasted_iota(jnp.int32, (1, BLOCK), 1)
            inside = (positions >= row_start) & (positions < row_end)
            scores = jnp.where(inside, scores, -1e30)
            new_top = jnp.maximum(top, jnp.max(scores, axis=1, keepdims=True))
            decay = jnp.exp(top - new_top)
            probs = jnp.exp(scores - new_top)
            new_total = total * decay + jnp.sum(probs, axis=1, keepdims=True)
            acc_ref[...] = acc_ref[...] * decay + lax.dot_general(
                probs.astype(BF16),
                keys_ref[:latent, pl.ds(offset, BLOCK)],
                (((1,), (1,)), ((), ())),
                preferred_element_type=F32,
            )
            return new_top, new_total

        _, total = lax.fori_loop(begin, end, step, (own_score, jnp.ones_like(own_score)))
        out_ref[rows, :] = (acc_ref[...] / total).astype(BF16)


def attend(bounds, queries, new_key, keys_t, latent):
    slots, heads, width = queries.shape
    rows = slots * heads
    return pl.pallas_call(
        attend_kernel,
        out_shape=jax.ShapeDtypeStruct((rows, latent), BF16),
        in_specs=[SMEM, VMEM, VMEM, VMEM],
        out_specs=VMEM,
        scratch_shapes=[pltpu.VMEM((2 * heads, latent), F32)],
        compiler_params=PARAMS,
        name="attend",
    )(bounds, queries.reshape(rows, width), new_key, keys_t)


def project_kernel(y_ref, latent_ref, up_ref, proj_ref, *refs):
    outs, values_ref, turned_ref = refs[:Y_SIZE], refs[Y_SIZE], refs[Y_SIZE + 1]
    head_v = up_ref.shape[2]
    both = jnp.concatenate([up_ref[0], up_ref[1]], axis=1)
    mapped = jnp.dot(latent_ref[...], both, preferred_element_type=F32)
    mapped = mapped.reshape(32, 2, 8, 2 * head_v)
    values_ref[...] = jnp.concatenate(
        [
            mapped[:, 0, :, :head_v].reshape(256, head_v),
            mapped[:, 1, :, head_v:].reshape(256, head_v),
        ],
        axis=1,
    ).astype(BF16)
    for k in range(Y_SIZE):
        source = pl.multiple_of(lax.rem(y_ref[0] + k, Y_SIZE) * 64, 64)
        turned_ref[64 * k : 64 * k + 64, :] = values_ref[pl.ds(source, 64), :]
    width = proj_ref.shape[1]
    for c in range(0, width, 512):
        part = jnp.dot(
            turned_ref[...], proj_ref[:, c : c + 512], preferred_element_type=F32
        ).astype(BF16)
        for k in range(Y_SIZE):
            outs[k][:, c : c + 512] = part[64 * k : 64 * k + 64]


def project(my_y, latent_rows, value_up, output_proj):
    width = output_proj.shape[1]
    return pl.pallas_call(
        project_kernel,
        out_shape=[jax.ShapeDtypeStruct((64, width), BF16)] * Y_SIZE,
        in_specs=[SMEM, VMEM, VMEM, VMEM],
        out_specs=[VMEM] * Y_SIZE,
        scratch_shapes=[pltpu.VMEM((256, 256), BF16), pltpu.VMEM((256, 256), BF16)],
        compiler_params=PARAMS,
        name="project",
    )(my_y, latent_rows, value_up, output_proj)


def feed_kernel(*refs):
    rows_refs = refs[:Y_SIZE]
    gate_ref, down_ref = refs[Y_SIZE], refs[Y_SIZE + 1]
    outs = refs[Y_SIZE + 2 : 2 * Y_SIZE + 2]
    normed_ref, hidden_ref = refs[2 * Y_SIZE + 2 :]
    parts, _, hidden_width, depth = gate_ref.shape
    for k in range(Y_SIZE):
        normed_ref[64 * k : 64 * k + 64, :] = rows_refs[k][...]
    contract = (((1,), (1,)), ((), ()))
    gate = jnp.zeros((256, hidden_width), F32)
    upward = jnp.zeros((256, hidden_width), F32)
    for d in range(parts):
        piece = normed_ref[:, d * depth : (d + 1) * depth]
        gate += lax.dot_general(piece, gate_ref[d, 0], contract, preferred_element_type=F32)
        upward += lax.dot_general(piece, gate_ref[d, 1], contract, preferred_element_type=F32)
    hidden_ref[...] = (gate / (1.0 + jnp.exp(-gate)) * upward).astype(BF16)
    width = down_ref.shape[1]
    for c in range(0, width, 512):
        part = jnp.dot(
            hidden_ref[...], down_ref[:, c : c + 512], preferred_element_type=F32
        ).astype(BF16)
        for k in range(Y_SIZE):
            outs[k][:, c : c + 512] = part[64 * k : 64 * k + 64]


def feed(row_blocks, gate_rows, down_proj):
    width = down_proj.shape[1]
    return pl.pallas_call(
        feed_kernel,
        out_shape=[jax.ShapeDtypeStruct((64, width), BF16)] * Y_SIZE,
        in_specs=[VMEM] * (Y_SIZE + 2),
        out_specs=[VMEM] * Y_SIZE,
        scratch_shapes=[
            pltpu.VMEM((256, width), BF16),
            pltpu.VMEM((256, down_proj.shape[0]), BF16),
        ],
        compiler_params=PARAMS,
        name="feed",
    )(*row_blocks, gate_rows, down_proj)


def sum_over_tp(blocks, direction):
    arrived = [blocks[0]] + [y_shift(blocks[k], direction * k) for k in (2, 1, 3)]
    column = sum(block.astype(F32) for block in arrived).astype(BF16)
    pieces = z_exchange(column).reshape(Z_SIZE, 8, column.shape[1])
    return jnp.sum(pieces.astype(F32), axis=0)


def local(
    queries,
    new_key,
    latent_cache,
    lengths,
    counts,
    residual,
    value_up,
    output_proj,
    norm_gain,
    gate_up,
    down_proj,
):
    slots, heads, _ = queries.shape
    latent = value_up.shape[1]
    gate_rows = lax.all_gather(gate_up.transpose(0, 2, 1), "dp", axis=0, tiled=False)

    live_mask = jnp.arange(slots, dtype=jnp.int32) < counts[0]
    used = jnp.where(live_mask, lengths, 0)
    bounds = jnp.concatenate([jnp.zeros((1,), jnp.int32), jnp.cumsum(used)])
    latent_out = attend(bounds, queries, new_key, latent_cache.T, latent)
    outgoing = latent_out.reshape(slots, heads, latent).transpose(1, 0, 2)
    outgoing = outgoing.reshape(32, 2 * slots, latent)
    incoming = lax.all_to_all(outgoing, "tp", split_axis=0, concat_axis=0, tiled=True)

    my_y = (lax.axis_index("tp") // Z_SIZE).astype(jnp.int32).reshape(1)
    terms = project(my_y, incoming.reshape(64 * slots, latent), value_up, output_proj)
    state = sum_over_tp(terms, 1) + residual
    mean_square = jnp.mean(state * state, axis=-1, keepdims=True)
    normed = (state * lax.rsqrt(mean_square + NORM_EPS) * norm_gain.astype(F32)).astype(BF16)

    column = z_exchange(jnp.tile(normed, (Z_SIZE, 1)))
    shifted = {k: y_shift(column, k) for k in (2, 1, 3)}
    blocks = [column] + [shifted[k] for k in (1, 2, 3)]
    terms = feed(blocks, gate_rows, down_proj)
    mixed = sum_over_tp(terms, -1) + state
    return jnp.where(live_mask[:, None], mixed, 0.0).astype(BF16)


def solution(mesh):
    placed = (
        P(("dp", "tp"), None, None),
        P(("dp", "tp"), None),
        P(("dp", "tp"), None),
        P(("dp", "tp")),
        P(("dp", "tp")),
        P(("dp", "tp"), None),
        P("tp", None, None),
        P("tp", None),
        P(),
        P(None, "dp", "tp"),
        P("tp", None),
    )
    return jax.shard_map(
        local, mesh=mesh, in_specs=placed, out_specs=P(("dp", "tp"), None), check_vma=False
    )
```

time: 526 us -> 200 us (0.38)
  waiting for transfers between devices: 392 us -> 108 us
  matrix products: 50.4 us -> 0 us
  local copies, waits for them, and re-layouts: 44.8 us -> 9.07 us
  starting transfers between devices: 10.1 us -> 34.2 us
  blocking collectives: 0 us -> 18.9 us
  Pallas kernels: 0 us -> 9.21 us
  other arithmetic: 9.87 us -> 4 us
    reduce_scatter x1 -> x0, waiting for transfers between devices: 218 us -> none  [local(): lax.psum_scatter(jnp.dot(piece, down_proj, preferred_element_type=jnp.flo...]
    psum x1 -> x0, waiting for transfers between devices: 156 us -> none  [local(): whole_state = lax.psum(terms, 'tp')]
    ppermute x0 -> x9, waiting for transfers between devices: none -> 57.6 us  [y_shift(): return lax.ppermute(array, 'tp', pairs)]
    dot_general x23 -> x0, matrix products: 50.4 us -> none  [the longest x12 24.3 us: block_scores(): lax.dot_general(query_rows, block_keys, (((1,), (1,)), ((), ())), preferr...]
    all_to_all x1 -> x3, waiting for transfers between devices: 17.6 us -> 49.6 us  [the longest x2 32.7 us: z_exchange(): lax.all_to_all(array, 'tp', split_axis=0, concat_axis=0, tiled=True, axis...]
    all_to_all x0 -> x1, blocking collectives: none -> 18.9 us  [z_exchange(): lax.all_to_all(array, 'tp', split_axis=0, concat_axis=0, tiled=True, axis...]
    unnamed x14 -> x22, local copies, waits for them, and re-layouts: 26.1 us -> 7.95 us
    all_to_all x1 -> x3, starting transfers between devices: 10 us -> 22.7 us  [the longest x1 13.2 us: local(): lax.all_to_all(outgoing, 'tp', split_axis=0, concat_axis=0, tiled=True)]
  transfers between devices with their start and end apart: 4 -> 13, of which waited for: 3 -> 10; matrix products, arithmetic and copies ran while one was open for 1% -> 2% of each run, Pallas kernels for 0% -> 3%
where the time goes in v1:
time: 200 us; the launch traced here: 198 us
  waiting for transfers between devices  108 us (54%)
  starting transfers between devices  34.2 us (17%)
  blocking collectives  18.9 us (9%)
  between operations  14.2 us (7%)
  Pallas kernels  9.21 us (5%)
  local copies, waits for them, and re-layouts  9.07 us (5%)
  other arithmetic  4 us (2%)
    ppermute x9, waiting for transfers between devices, y_shift(): return lax.ppermute(array, 'tp', pairs)  57.6 us
    all_to_all x2, waiting for transfers between devices, z_exchange(): lax.all_to_all(array, 'tp', split_axis=0, concat_axis=0, tiled=True, axis...  32.7 us
    all_to_all x1, blocking collectives, z_exchange(): lax.all_to_all(array, 'tp', split_axis=0, concat_axis=0, tiled=True, axis...  18.9 us
    all_to_all x1, waiting for transfers between devices, local(): lax.all_to_all(outgoing, 'tp', split_axis=0, concat_axis=0, tiled=True)  16.9 us
    all_to_all x1, starting transfers between devices, local(): lax.all_to_all(outgoing, 'tp', split_axis=0, concat_axis=0, tiled=True)  13.2 us
    ppermute x9, starting transfers between devices, y_shift(): return lax.ppermute(array, 'tp', pairs)  11.6 us
    all_to_all x2, starting transfers between devices, z_exchange(): lax.all_to_all(array, 'tp', split_axis=0, concat_axis=0, tiled=True, axis...  9.45 us
    unnamed x22, local copies, waits for them, and re-layouts  7.95 us
  transfers between devices with their start and end apart: 13, of which 10 were waited for; matrix products, arithmetic and copies ran while one was open for 2% of the time, Pallas kernels for 3%

profile of v1, /device:TPU:2, one launch (start us, length us, event | category | flops | bytes accessed | tf_op | source)
XLA Modules:
  0.0 197.6 jit_solution(2178077442363507591)
XLA Ops:
  8.8 2.0 %copy-done.1 = bf16[3072,576]{0,1:T(8,128)(2,1)S(1)} copy-done((bf16[3072,576]{0,1:T(8,128)(2,1)S(1)}, bf16[3072,576]{0,1:T(8,128)(2,1)}, u32[]{:S(2)}) %copy-start.1) | copy-done | bytes 3538968
  12.6 4.6 %attend.1 = bf16[512,512]{1,0:T(8,128)(2,1)S(1)} custom-call(s32[9]{0:T(128)S(1)} %pad_add_fusion.bounds_ref, bf16[512,576]{1,0:T(8,128)(2,1)S(1)} %bitcast.29, bf16[8,576]{1,0:T(8,128)(2,1)S(1)} %copy-done.8, bf16[576,3072]{1,0:T(8,128)(2,1)S(1)} %bitcast.22), custom_call_target="tpu_custom_call" | custom-call | tf_op jit(solution)/shard_map/attend/pallas_call | solution.py:90
  18.3 13.2 %all-to-all-start = ((bf16[32,16,512]{2,1,0:T(8,128)(2,1)}), bf16[32,16,512]{2,1,0:T(8,128)(2,1)S(1)}, u32[]{:S(2)}, u32[]{:S(2)}) async-start(bf16[32,16,512]{2,1,0:T(8,128)(2,1)} %bitcast.8), calls=%async_computation | async-start | bytes 1048576 | tf_op jit(solution)/shard_map/all_to_all | solution.py:210
  31.6 16.9 %all-to-all-done = bf16[32,16,512]{2,1,0:T(8,128)(2,1)S(1)} async-done(((bf16[32,16,512]{2,1,0:T(8,128)(2,1)}), bf16[32,16,512]{2,1,0:T(8,128)(2,1)S(1)}, u32[]{:S(2)}, u32[]{:S(2)}) %all-to-all-start) | async-done | bytes 524320 | tf_op jit(solution)/shard_map/all_to_all | solution.py:210
  49.6 1.2 collective-permute-start
  51.4 2.7 %collective-permute-start.2 = (bf16[64,3584]{1,0:T(8,128)(2,1)S(1)}, bf16[64,3584]{1,0:T(8,128)(2,1)S(1)}, u32[]{:S(2)}, u32[]{:S(2)}) collective-permute-start(bf16[64,3584]{1,0:T(8,128)(2,1)S(1)} %get-tuple-element.16), channel_id=1, source_target_pairs={{0,24},{1,25},{2,26},{3,27},{4,28},{5,29},{6,30},{7,31},{8,0},{9,1... | collective-permute-start | bytes 1376264 | tf_op jit(solution)/shard_map/ppermute | solution.py:29
  54.1 10.6 %collective-permute-done = bf16[64,3584]{1,0:T(8,128)(2,1)S(1)} collective-permute-done((bf16[64,3584]{1,0:T(8,128)(2,1)S(1)}, bf16[64,3584]{1,0:T(8,128)(2,1)S(1)}, u32[]{:S(2)}, u32[]{:S(2)}) %collective-permute-start) | collective-permute-done | bytes 458784 | tf_op jit(solution)/shard_map/ppermute | solution.py:29
  64.7 4.9 %collective-permute-done.1 = bf16[64,3584]{1,0:T(8,128)(2,1)S(1)} collective-permute-done((bf16[64,3584]{1,0:T(8,128)(2,1)S(1)}, bf16[64,3584]{1,0:T(8,128)(2,1)S(1)}, u32[]{:S(2)}, u32[]{:S(2)}) %collective-permute-start.1) | collective-permute-done | bytes 458784 | tf_op jit(solution)/shard_map/ppermute | solution.py:29
  70.6 6.0 %all-to-all-start.1 = ((bf16[8,8,3584]{2,1,0:T(8,128)(2,1)}), bf16[8,8,3584]{2,1,0:T(8,128)(2,1)S(1)}, u32[]{:S(2)}, u32[]{:S(2)}) async-start(bf16[8,8,3584]{2,1,0:T(8,128)(2,1)} %fusion), calls=%async_computation.1 | async-start | bytes 917504 | tf_op jit(solution)/shard_map/all_to_all | solution.py:33
  76.6 16.3 %all-to-all-done.1 = bf16[8,8,3584]{2,1,0:T(8,128)(2,1)S(1)} async-done(((bf16[8,8,3584]{2,1,0:T(8,128)(2,1)}), bf16[8,8,3584]{2,1,0:T(8,128)(2,1)S(1)}, u32[]{:S(2)}, u32[]{:S(2)}) %all-to-all-start.1) | async-done | bytes 458784 | tf_op jit(solution)/shard_map/all_to_all | solution.py:33
  93.2 18.9 %all_to_all.31 = bf16[8,8,3584]{2,1,0:T(8,128)(2,1)S(1)} all-to-all(bf16[8,8,3584]{2,1,0:T(8,128)(2,1)S(1)} %tile.2), channel_id=1, replica_groups={{0,1,2,3,4,5,6,7},{8,9,10,11,12,13,14,15},{16,17,18,19,20,21,22,23},{24..., dimensions={0} | all-to-all | bytes 917504 | tf_op jit(solution)/shard_map/all_to_all | solution.py:33
  112.1 2.0 %collective-permute-start.5 = (bf16[64,3584]{1,0:T(8,128)(2,1)S(1)}, bf16[64,3584]{1,0:T(8,128)(2,1)S(1)}, u32[]{:S(2)}, u32[]{:S(2)}) collective-permute-start(bf16[64,3584]{1,0:T(8,128)(2,1)S(1)} %bitcast.25), channel_id=1, source_target_pairs={{0,24},{1,25},{2,26},{3,27},{4,28},{5,29},{6,30},{7,31},{8,0},{9,1... | collective-permute-start | bytes 1376264 | tf_op jit(solution)/shard_map/ppermute | solution.py:29
  114.2 1.5 collective-permute-start.4
  115.7 18.2 %collective-permute-done.5.refs_3_ = bf16[64,3584]{1,0:T(8,128)(2,1)S(1)} collective-permute-done((bf16[64,3584]{1,0:T(8,128)(2,1)S(1)}, bf16[64,3584]{1,0:T(8,128)(2,1)S(1)}, u32[]{:S(2)}, u32[]{:S(2)}) %collective-permute-start.5) | collective-permute-done | bytes 458784 | tf_op jit(solution)/shard_map/ppermute | solution.py:29
  133.9 3.7 %collective-permute-done.3.refs_1_ = bf16[64,3584]{1,0:T(8,128)(2,1)S(1)} collective-permute-done((bf16[64,3584]{1,0:T(8,128)(2,1)S(1)}, bf16[64,3584]{1,0:T(8,128)(2,1)S(1)}, u32[]{:S(2)}, u32[]{:S(2)}) %collective-permute-start.3) | collective-permute-done | bytes 458784 | tf_op jit(solution)/shard_map/ppermute | solution.py:29
  138.3 2.3 %copy-done = bf16[16,288,448]{2,1,0:T(8,128)(2,1)S(1)} copy-done((bf16[16,288,448]{2,1,0:T(8,128)(2,1)S(1)}, bf16[16,288,448]{2,1,0:T(8,128)(2,1)}, u32[]{:S(2)}) %copy-start) | copy-done | bytes 4128792
  141.7 3.5 %feed.1 = (bf16[64,3584]{1,0:T(8,128)(2,1)S(1)}, bf16[64,3584]{1,0:T(8,128)(2,1)S(1)}, bf16[64,3584]{1,0:T(8,128)(2,1)S(1)}, bf16[64,3584]{1,0:T(8,128)(2,1)S(1)}) custom-call(bf16[64,3584]{1,0:T(8,128)(2,1)S(1)} %bitcast.28, bf16[64,3584]{1,0:T(8,128)(2,1)S(1)} %copy-done.6, bf16[64,3584]{1,0:T(8,128)(2,1)S(1)} %collective-permute-done.4.refs_2_, ...), custom_call_target="tpu_custom_call" | custom-call | tf_op jit(solution)/shard_map/feed/pallas_call | solution.py:166
  145.2 1.6 collective-permute-start.6
  146.7 1.2 collective-permute-start.7
  148.8 11.4 %collective-permute-done.6 = bf16[64,3584]{1,0:T(8,128)(2,1)S(1)} collective-permute-done((bf16[64,3584]{1,0:T(8,128)(2,1)S(1)}, bf16[64,3584]{1,0:T(8,128)(2,1)S(1)}, u32[]{:S(2)}, u32[]{:S(2)}) %collective-permute-start.6) | collective-permute-done | bytes 458784 | tf_op jit(solution)/shard_map/ppermute | solution.py:29
  160.2 5.8 %collective-permute-done.7 = bf16[64,3584]{1,0:T(8,128)(2,1)S(1)} collective-permute-done((bf16[64,3584]{1,0:T(8,128)(2,1)S(1)}, bf16[64,3584]{1,0:T(8,128)(2,1)S(1)}, u32[]{:S(2)}, u32[]{:S(2)}) %collective-permute-start.7) | collective-permute-done | bytes 458784 | tf_op jit(solution)/shard_map/ppermute | solution.py:29
  165.9 3.1 %collective-permute-done.8 = bf16[64,3584]{1,0:T(8,128)(2,1)S(1)} collective-permute-done((bf16[64,3584]{1,0:T(8,128)(2,1)S(1)}, bf16[64,3584]{1,0:T(8,128)(2,1)S(1)}, u32[]{:S(2)}, u32[]{:S(2)}) %collective-permute-start.8) | collective-permute-done | bytes 458784 | tf_op jit(solution)/shard_map/ppermute | solution.py:29
  170.0 3.5 %all-to-all-start.3 = ((bf16[8,8,3584]{2,1,0:T(8,128)(2,1)}), bf16[8,8,3584]{2,1,0:T(8,128)(2,1)S(1)}, u32[]{:S(2)}, u32[]{:S(2)}) async-start(bf16[8,8,3584]{2,1,0:T(8,128)(2,1)} %fusion.1), calls=%async_computation.3 | async-start | bytes 917504 | tf_op jit(solution)/shard_map/all_to_all | solution.py:33
  173.5 16.5 %all-to-all-done.3 = bf16[8,8,3584]{2,1,0:T(8,128)(2,1)S(1)} async-done(((bf16[8,8,3584]{2,1,0:T(8,128)(2,1)}), bf16[8,8,3584]{2,1,0:T(8,128)(2,1)S(1)}, u32[]{:S(2)}, u32[]{:S(2)}) %all-to-all-start.3) | async-done | bytes 458784 | tf_op jit(solution)/shard_map/all_to_all | solution.py:33
  (44 shorter events, 11.9 us)
Async XLA Ops:
  6.5 131.8 %all-gather.3.cloned.1.call-start = ((), (), s32[]{:S(2)}) async-start(), calls=%async_computation.4 | async-start | bytes 5308416 | tf_op jit(solution)/shard_map/all_gather | solution.py:202
  6.5 41.9 %copy-start.7 = (bf16[2,512,128]{2,1,0:T(8,128)(2,1)S(1)}, bf16[2,512,128]{2,1,0:T(8,128)(2,1)}, u32[]{:S(2)}) copy-start(bf16[2,512,128]{2,1,0:T(8,128)(2,1)} %up_ref.1) | copy-start | bytes 786436
  8.8 2.0 %copy-start.1 = (bf16[3072,576]{0,1:T(8,128)(2,1)S(1)}, bf16[3072,576]{0,1:T(8,128)(2,1)}, u32[]{:S(2)}) copy-start(bf16[3072,576]{0,1:T(8,128)(2,1)} %param.13) | copy-start | bytes 10616836
  10.8 1.1 copy-start.4
  11.9 0.7 copy-start.8
  12.6 35.9 %copy-start.3 = (bf16[256,3584]{1,0:T(8,128)(2,1)S(1)}, bf16[256,3584]{1,0:T(8,128)(2,1)}, u32[]{:S(2)}) copy-start(bf16[256,3584]{1,0:T(8,128)(2,1)} %proj_ref.1) | copy-start | bytes 5505028
  18.3 58.2 %copy-start.10 = (bf16[3584]{0:T(1024)(128)(2,1)S(1)}, bf16[3584]{0:T(1024)(128)(2,1)}, u32[]{:S(2)}) copy-start(bf16[3584]{0:T(1024)(128)(2,1)} %param.19) | copy-start | bytes 21508
  18.3 74.6 %copy-start.9 = (f32[8,3584]{1,0:T(8,128)S(1)}, f32[8,3584]{1,0:T(8,128)}, u32[]{:S(2)}) copy-start(f32[8,3584]{1,0:T(8,128)} %param.16) | copy-start | bytes 344068
  18.3 30.2 %all-to-all-start = ((bf16[32,16,512]{2,1,0:T(8,128)(2,1)}), bf16[32,16,512]{2,1,0:T(8,128)(2,1)S(1)}, u32[]{:S(2)}, u32[]{:S(2)}) async-start(bf16[32,16,512]{2,1,0:T(8,128)(2,1)} %bitcast.8), calls=%async_computation | async-start | bytes 1048576 | tf_op jit(solution)/shard_map/all_to_all | solution.py:210
  49.6 88.7 %copy-start.2 = (bf16[288,3584]{1,0:T(8,128)(2,1)S(1)}, bf16[288,3584]{1,0:T(8,128)(2,1)}, u32[]{:S(2)}) copy-start(bf16[288,3584]{1,0:T(8,128)(2,1)} %refs_5_.1) | copy-start | bytes 6193156
  49.6 15.0 %collective-permute-start = (bf16[64,3584]{1,0:T(8,128)(2,1)S(1)}, bf16[64,3584]{1,0:T(8,128)(2,1)S(1)}, u32[]{:S(2)}, u32[]{:S(2)}) collective-permute-start(bf16[64,3584]{1,0:T(8,128)(2,1)S(1)} %get-tuple-element.14), channel_id=1, source_target_pairs={{0,16},{1,17},{2,18},{3,19},{4,20},{5,21},{6,22},{7,23},{8,24},{9,... | collective-permute-start | bytes 1376264 | tf_op jit(solution)/shard_map/ppermute | solution.py:29
  50.9 18.7 %collective-permute-start.1 = (bf16[64,3584]{1,0:T(8,128)(2,1)S(1)}, bf16[64,3584]{1,0:T(8,128)(2,1)S(1)}, u32[]{:S(2)}, u32[]{:S(2)}) collective-permute-start(bf16[64,3584]{1,0:T(8,128)(2,1)S(1)} %get-tuple-element.15), channel_id=1, source_target_pairs={{0,8},{1,9},{2,10},{3,11},{4,12},{5,13},{6,14},{7,15},{8,16},{9,17... | collective-permute-start | bytes 1376264 | tf_op jit(solution)/shard_map/ppermute | solution.py:29
  51.4 18.2 %collective-permute-start.2 = (bf16[64,3584]{1,0:T(8,128)(2,1)S(1)}, bf16[64,3584]{1,0:T(8,128)(2,1)S(1)}, u32[]{:S(2)}, u32[]{:S(2)}) collective-permute-start(bf16[64,3584]{1,0:T(8,128)(2,1)S(1)} %get-tuple-element.16), channel_id=1, source_target_pairs={{0,24},{1,25},{2,26},{3,27},{4,28},{5,29},{6,30},{7,31},{8,0},{9,1... | collective-permute-start | bytes 1376264 | tf_op jit(solution)/shard_map/ppermute | solution.py:29
  70.6 22.3 %all-to-all-start.1 = ((bf16[8,8,3584]{2,1,0:T(8,128)(2,1)}), bf16[8,8,3584]{2,1,0:T(8,128)(2,1)S(1)}, u32[]{:S(2)}, u32[]{:S(2)}) async-start(bf16[8,8,3584]{2,1,0:T(8,128)(2,1)} %fusion), calls=%async_computation.1 | async-start | bytes 917504 | tf_op jit(solution)/shard_map/all_to_all | solution.py:33
  112.1 21.7 %collective-permute-start.5 = (bf16[64,3584]{1,0:T(8,128)(2,1)S(1)}, bf16[64,3584]{1,0:T(8,128)(2,1)S(1)}, u32[]{:S(2)}, u32[]{:S(2)}) collective-permute-start(bf16[64,3584]{1,0:T(8,128)(2,1)S(1)} %bitcast.25), channel_id=1, source_target_pairs={{0,24},{1,25},{2,26},{3,27},{4,28},{5,29},{6,30},{7,31},{8,0},{9,1... | collective-permute-start | bytes 1376264 | tf_op jit(solution)/shard_map/ppermute | solution.py:29
  114.2 19.7 %collective-permute-start.4 = (bf16[64,3584]{1,0:T(8,128)(2,1)S(1)}, bf16[64,3584]{1,0:T(8,128)(2,1)S(1)}, u32[]{:S(2)}, u32[]{:S(2)}) collective-permute-start(bf16[64,3584]{1,0:T(8,128)(2,1)S(1)} %bitcast.26), channel_id=1, source_target_pairs={{0,16},{1,17},{2,18},{3,19},{4,20},{5,21},{6,22},{7,23},{8,24},{9,... | collective-permute-start | bytes 1376264 | tf_op jit(solution)/shard_map/ppermute | solution.py:29
  115.7 21.9 %collective-permute-start.3 = (bf16[64,3584]{1,0:T(8,128)(2,1)S(1)}, bf16[64,3584]{1,0:T(8,128)(2,1)S(1)}, u32[]{:S(2)}, u32[]{:S(2)}) collective-permute-start(bf16[64,3584]{1,0:T(8,128)(2,1)S(1)} %bitcast.27), channel_id=1, source_target_pairs={{0,8},{1,9},{2,10},{3,11},{4,12},{5,13},{6,14},{7,15},{8,16},{9,17... | collective-permute-start | bytes 1376264 | tf_op jit(solution)/shard_map/ppermute | solution.py:29
  137.5 0.8 copy-start.5
  138.3 2.3 %copy-start = (bf16[16,288,448]{2,1,0:T(8,128)(2,1)S(1)}, bf16[16,288,448]{2,1,0:T(8,128)(2,1)}, u32[]{:S(2)}) copy-start(bf16[16,288,448]{2,1,0:T(8,128)(2,1)} %all-gather.3.cloned.1.call-done) | copy-start | bytes 12386308
  140.7 1.0 copy-start.6
  145.2 15.0 %collective-permute-start.6 = (bf16[64,3584]{1,0:T(8,128)(2,1)S(1)}, bf16[64,3584]{1,0:T(8,128)(2,1)S(1)}, u32[]{:S(2)}, u32[]{:S(2)}) collective-permute-start(bf16[64,3584]{1,0:T(8,128)(2,1)S(1)} %get-tuple-element.18), channel_id=1, source_target_pairs={{0,16},{1,17},{2,18},{3,19},{4,20},{5,21},{6,22},{7,23},{8,24},{9,... | collective-permute-start | bytes 1376264 | tf_op jit(solution)/shard_map/ppermute | solution.py:29
  146.7 19.2 %collective-permute-start.7 = (bf16[64,3584]{1,0:T(8,128)(2,1)S(1)}, bf16[64,3584]{1,0:T(8,128)(2,1)S(1)}, u32[]{:S(2)}, u32[]{:S(2)}) collective-permute-start(bf16[64,3584]{1,0:T(8,128)(2,1)S(1)} %get-tuple-element.19), channel_id=1, source_target_pairs={{0,24},{1,25},{2,26},{3,27},{4,28},{5,29},{6,30},{7,31},{8,0},{9,1... | collective-permute-start | bytes 1376264 | tf_op jit(solution)/shard_map/ppermute | solution.py:29
  147.9 21.1 %collective-permute-start.8 = (bf16[64,3584]{1,0:T(8,128)(2,1)S(1)}, bf16[64,3584]{1,0:T(8,128)(2,1)S(1)}, u32[]{:S(2)}, u32[]{:S(2)}) collective-permute-start(bf16[64,3584]{1,0:T(8,128)(2,1)S(1)} %get-tuple-element.20), channel_id=1, source_target_pairs={{0,8},{1,9},{2,10},{3,11},{4,12},{5,13},{6,14},{7,15},{8,16},{9,17... | collective-permute-start | bytes 1376264 | tf_op jit(solution)/shard_map/ppermute | solution.py:29
  170.0 19.9 %all-to-all-start.3 = ((bf16[8,8,3584]{2,1,0:T(8,128)(2,1)}), bf16[8,8,3584]{2,1,0:T(8,128)(2,1)S(1)}, u32[]{:S(2)}, u32[]{:S(2)}) async-start(bf16[8,8,3584]{2,1,0:T(8,128)(2,1)} %fusion.1), calls=%async_computation.3 | async-start | bytes 917504 | tf_op jit(solution)/shard_map/all_to_all | solution.py:33
Sparse Core Ops, SparseCore 0:
  9.2 38.8 all-gather.2
